TPU v7x, 512 devices: a whole 4x4x16 slice. The times are simulated.
512 devices in a mesh: dp: 64 (over z, x), group: 8 (over y, core).
Axes of the slice: x: 4, y: 4, z: 16, core: 2. Of those that a mesh axis runs over, the one named last changes fastest.
Arguments:
- query_hidden: bfloat16 [4096, 4096], P(('dp', 'group')), may hold values from -0.2 to 0.2
- passage_hidden: bfloat16 [16384, 4096], P(('dp', 'group')), may hold values from -0.2 to 0.2
- projection: bfloat16 [4096, 4096], P(None, 'group'), may hold values from -0.09375 to 0.09375
- negative_ids: int32 [4096, 16], replicated, may hold values from 0 to 16383, as said below
Outputs:
- query_loss: float32 [4096], P(('dp', 'group'))
- query_hidden_grad: bfloat16 [4096, 4096], P(('dp', 'group'))
- passage_hidden_grad: bfloat16 [16384, 4096], P(('dp', 'group'))
Inputs may be any that keep to these rules, and one draw needn't show every extreme that they name: `negative_ids`: take the 64 queries of one index of dp, rows a * 64 to (a + 1) * 64 - 1. Of their 1024 ids, at most 32 name passages of any one index o of dp (ids o * 256 to (o + 1) * 256 - 1), and some index of dp receives exactly 32 from every index of dp.
All inputs are finite; a program needn't handle non-finite values.
Results may differ from a plain program's by a relative error of at most 0.017.
Values may be sent and summed in bfloat16 or wider, within the bound.
A program may use at most 64 MiB of HBM per device.

v0:
```python
import jax
import jax.numpy as jnp
from jax import lax
from jax.sharding import PartitionSpec as P

SOFTMAX_TEMP_SCALE = 0.05
EPSILON = 1e-06


def prior_counts(flags):
    total_rows = flags.shape[0]
    positions = jnp.arange(total_rows, dtype=jnp.int32)
    lower = (positions[None, :] < positions[:, None]).astype(jnp.bfloat16)
    earlier = jnp.dot(lower, flags.astype(jnp.bfloat16), preferred_element_type=jnp.float32)
    return earlier.astype(jnp.int32)


def request_slots(owner_ids, peer_count):
    matches = (owner_ids[:, None] == jnp.arange(peer_count, dtype=jnp.int32)[None, :]).astype(
        jnp.int32
    )
    earlier = prior_counts(matches)
    return jnp.sum(earlier * matches, axis=1)


def per_device(query_hidden, passage_hidden, projection, negative_ids):
    groups = lax.axis_size("group")
    peer_count = lax.axis_size("dp")
    my_peer = lax.axis_index("dp")
    my_member = lax.axis_index("group")
    query_rows = query_hidden.shape[0]
    passage_rows = passage_hidden.shape[0]
    device_rows = query_rows + passage_rows
    per_query = passage_rows // query_rows
    columns = projection.shape[1]
    neg_count = negative_ids.shape[1]
    group_queries = groups * query_rows
    group_passages = groups * passage_rows
    requests = group_queries * neg_count
    capacity = 2 * requests // peer_count
    slot_total = peer_count * capacity
    own_rows = jnp.concatenate([query_hidden, passage_hidden], axis=0)
    projected = jnp.dot(
        lax.all_gather(own_rows, "group", axis=0, tiled=True),
        projection,
        preferred_element_type=jnp.float32,
    ).astype(jnp.bfloat16)
    blocks = projected.reshape(groups, device_rows, columns)
    proj_query = blocks[:, :query_rows].reshape(group_queries, columns)
    proj_passage = blocks[:, query_rows:].reshape(group_passages, columns)
    my_ids = lax.dynamic_slice_in_dim(
        negative_ids, my_peer * group_queries, group_queries, 0
    ).reshape(requests)
    my_owner = my_ids // group_passages
    my_slot = request_slots(my_owner, peer_count)
    query_of_request = jnp.arange(requests, dtype=jnp.int32) // neg_count
    slot_of_request = my_owner * capacity + my_slot
    slot_hits = slot_of_request[:, None] == jnp.arange(slot_total, dtype=jnp.int32)[None, :]
    request_of_slot = jnp.sum(
        jnp.where(slot_hits, jnp.arange(requests, dtype=jnp.int32)[:, None], 0), axis=0
    )
    slot_filled = jnp.any(slot_hits, axis=0)
    query_of_slot = query_of_request[request_of_slot]
    all_ids = negative_ids.reshape(peer_count, requests)
    is_mine = all_ids // group_passages == my_peer
    mine_count = is_mine.astype(jnp.int32)
    slot_rank = prior_counts(mine_count.T).T
    rank_hits = is_mine[:, :, None] & (
        slot_rank[:, :, None] == jnp.arange(capacity, dtype=jnp.int32)[None, None, :]
    )
    asked_local = jnp.sum(jnp.where(rank_hits, (all_ids % group_passages)[:, :, None], 0), axis=1)
    outgoing = jnp.take(proj_passage, asked_local, axis=0)
    fetched = lax.all_to_all(outgoing, "dp", split_axis=0, concat_axis=0, tiled=True)
    neg_rows = fetched.reshape(slot_total, columns)[slot_of_request].reshape(
        group_queries, neg_count, columns
    )
    inner_in = jnp.dot(proj_query, proj_passage.T, preferred_element_type=jnp.float32)
    inner_neg = jnp.einsum("qc,qkc->qk", proj_query, neg_rows, preferred_element_type=jnp.float32)
    square_query = jnp.einsum(
        "qc,qc->q", proj_query, proj_query, preferred_element_type=jnp.float32
    )
    square_passage = jnp.einsum(
        "pc,pc->p", proj_passage, proj_passage, preferred_element_type=jnp.float32
    )
    square_neg = jnp.einsum("qkc,qkc->qk", neg_rows, neg_rows, preferred_element_type=jnp.float32)
    inner_in, inner_neg, square_query, square_passage, square_neg = lax.psum(
        (inner_in, inner_neg, square_query, square_passage, square_neg), "group"
    )
    norm_query = jnp.sqrt(square_query + EPSILON)
    norm_passage = jnp.sqrt(square_passage + EPSILON)
    norm_neg = jnp.sqrt(square_neg + EPSILON)
    cosine_positive_pair = inner_in / (norm_query[:, None] * norm_passage[None, :])
    cosine_negative_pair = inner_neg / (norm_query[:, None] * norm_neg)
    positive_weight = jnp.exp((cosine_positive_pair - 1.0) / SOFTMAX_TEMP_SCALE)
    negative_weight = jnp.exp((cosine_negative_pair - 1.0) / SOFTMAX_TEMP_SCALE)
    summed_weight = jnp.sum(positive_weight, axis=1) + jnp.sum(negative_weight, axis=1)
    positive_passage = (
        jnp.arange(group_passages, dtype=jnp.int32)[None, :]
        == (jnp.arange(group_queries, dtype=jnp.int32) * per_query)[:, None]
    ).astype(jnp.float32)
    loss_values = (
        jnp.log(summed_weight)
        + (1.0 - jnp.sum(positive_passage * cosine_positive_pair, axis=1)) / SOFTMAX_TEMP_SCALE
    )
    positive_slope = (
        positive_weight / summed_weight[:, None] - positive_passage
    ) / SOFTMAX_TEMP_SCALE
    negative_slope = negative_weight / summed_weight[:, None] / SOFTMAX_TEMP_SCALE
    radial_query = jnp.sum(positive_slope * cosine_positive_pair, axis=1) + jnp.sum(
        negative_slope * cosine_negative_pair, axis=1
    )
    radial_passage = jnp.sum(positive_slope * cosine_positive_pair, axis=0)
    radial_neg = (negative_slope * cosine_negative_pair).reshape(requests)
    coef_in = (positive_slope / (norm_query[:, None] * norm_passage[None, :])).astype(jnp.bfloat16)
    coef_neg = (negative_slope / (norm_query[:, None] * norm_neg)).astype(jnp.bfloat16)
    grad_query = (
        jnp.dot(coef_in, proj_passage, preferred_element_type=jnp.float32)
        + jnp.einsum("qk,qkc->qc", coef_neg, neg_rows, preferred_element_type=jnp.float32)
        - (radial_query / (square_query + EPSILON))[:, None] * proj_query.astype(jnp.float32)
    )
    grad_passage = jnp.dot(coef_in.T, proj_query, preferred_element_type=jnp.float32)
    neg_coef = coef_neg.reshape(requests).astype(jnp.float32)
    slot_radial = jnp.where(slot_filled, radial_neg[request_of_slot], 0.0).reshape(
        peer_count, capacity
    )
    slot_coef_flat = jnp.where(slot_filled, neg_coef[request_of_slot], 0.0)
    slot_rows = (slot_coef_flat[:, None] * proj_query[query_of_slot].astype(jnp.float32)).reshape(
        peer_count, capacity, columns
    )
    contribution, got_radial = (
        lax.all_to_all(
            slot_rows.astype(jnp.bfloat16), "dp", split_axis=0, concat_axis=0, tiled=True
        ).astype(slot_rows.dtype),
        lax.all_to_all(
            slot_radial.astype(jnp.bfloat16), "dp", split_axis=0, concat_axis=0, tiled=True
        ).astype(slot_radial.dtype),
    )
    flat_local = asked_local.reshape(slot_total)
    owner_table = (
        jnp.arange(group_passages, dtype=jnp.int32)[:, None] == flat_local[None, :]
    ).astype(jnp.float32)
    grad_passage = grad_passage + jnp.dot(
        owner_table,
        contribution.reshape(slot_total, columns),
        precision=lax.Precision.HIGHEST,
        preferred_element_type=jnp.float32,
    )
    radial_passage = radial_passage + jnp.dot(
        owner_table,
        got_radial.reshape(slot_total),
        precision=lax.Precision.HIGHEST,
        preferred_element_type=jnp.float32,
    )
    grad_passage = grad_passage - (radial_passage / (square_passage + EPSILON))[
        :, None
    ] * proj_passage.astype(jnp.float32)
    down_query = grad_query.astype(jnp.bfloat16).reshape(groups, query_rows, columns)
    down_passage = grad_passage.astype(jnp.bfloat16).reshape(groups, passage_rows, columns)
    stacked = jnp.concatenate([down_query, down_passage], axis=1).reshape(
        groups * device_rows, columns
    )
    hidden_grad = lax.psum_scatter(
        lax.dot_general(
            stacked, projection, (((1,), (1,)), ((), ())), preferred_element_type=jnp.float32
        ).astype(jnp.bfloat16),
        "group",
        scatter_dimension=0,
        tiled=True,
    )
    loss_rows = lax.dynamic_slice_in_dim(loss_values, my_member * query_rows, query_rows, 0)
    return (loss_rows, hidden_grad[:query_rows], hidden_grad[query_rows:])


def solution(mesh):
    in_specs = (P(("dp", "group"), None), P(("dp", "group"), None), P(None, "group"), P())
    out_specs = (P(("dp", "group")), P(("dp", "group"), None), P(("dp", "group"), None))
    return jax.shard_map(
        per_device, mesh=mesh, in_specs=in_specs, out_specs=out_specs, check_vma=False
    )
```

profile of v0, /device:TPU:1, one launch (start us, length us, event | category | flops | bytes accessed | tf_op | source)
XLA Modules:
  0.0 402.0 jit_solution(17985937429985390604)
XLA Ops:
  7.2 1.7 pad_maximum_fusion
  8.9 1.5 copy.14
  10.5 1.6 reshape.318
  12.9 2.4 select_reduce_fusion.1
  15.4 34.3 %all-gather.2.cloned.1.call-done = bf16[320,4096]{1,0:T(8,128)(2,1)} async-done(((bf16[40,4096]{1,0:T(8,128)(2,1)}), bf16[320,4096]{1,0:T(8,128)(2,1)}) %all-gather.2.cloned.1.call-update) | async-done | bytes 2621456 | tf_op jit(solution)/shard_map/all_gather | solution.py:44
  49.7 4.5 %convolution_convert_fusion.1 = bf16[320,512]{1,0:T(8,128)(2,1)S(1)} fusion(bf16[320,4096]{1,0:T(8,128)(2,1)} %all-gather.2.cloned.1.call-done, bf16[4096,512]{1,0:T(8,128)(2,1)} %param.6), kind=kOutput, calls=%fused_computation.26 | convolution fusion | flops 1342341120 | bytes 7143424 | tf_op jit(solution)/shard_map/dot_general | solution.py:43
  54.2 7.5 %gather_fusion = bf16[2048,512]{1,0:T(8,128)(2,1)S(1)} fusion(bf16[256,512]{1,0:T(8,128)(2,1)S(1)} %bitcast.50, s32[2048]{0:T(1024)S(1)} %broadcast_clamp_fusion.2), kind=kCustom, calls=%fused_computation | custom fusion | bytes 4202496 | tf_op jit(solution)/shard_map/jit(_take)/gather | solution.py:72
  63.3 15.3 %all-to-all-start = ((bf16[64,32,512]{2,1,0:T(8,128)(2,1)}), bf16[64,32,512]{2,1,0:T(8,128)(2,1)S(1)}, u32[]{:S(2)}, u32[]{:S(2)}) async-start(bf16[64,32,512]{2,1,0:T(8,128)(2,1)} %broadcast_select_fusion), calls=%async_computation | async-start | bytes 4194304 | tf_op jit(solution)/shard_map/all_to_all | solution.py:73
  81.7 8.6 %gather_fusion.3 = s32[2048]{0:T(1024)S(1)} fusion(s32[1024]{0:T(1024)S(1)} %add_select_fusion.2, s32[2048]{0:T(1024)S(1)} %broadcast_clamp_fusion.1), kind=kCustom, calls=%fused_computation.3 | custom fusion | bytes 24576 | tf_op jit(solution)/shard_map/gather | solution.py:63
  92.7 9.2 %gather_fusion.4 = bf16[2048,512]{1,0:T(8,128)(2,1)} fusion(bf16[64,512]{1,0:T(8,128)(2,1)S(1)} %get-tuple-element.15, s32[2048]{0:T(1024)S(1)} %broadcast_clamp_fusion), kind=kCustom, calls=%fused_computation.4 | custom fusion | bytes 4202496 | tf_op jit(solution)/shard_map/gather | solution.py:127
  102.1 73.6 %all-to-all-done = bf16[64,32,512]{2,1,0:T(8,128)(2,1)S(1)} async-done(((bf16[64,32,512]{2,1,0:T(8,128)(2,1)}), bf16[64,32,512]{2,1,0:T(8,128)(2,1)S(1)}, u32[]{:S(2)}, u32[]{:S(2)}) %all-to-all-start) | async-done | bytes 2097184 | tf_op jit(solution)/shard_map/all_to_all | solution.py:73
  175.7 4.0 gather_fusion.1
  180.4 25.3 %all-reduce = (f32[256]{0:T(256)S(1)}, f32[64]{0:T(128)S(1)}, f32[64,16]{1,0:T(8,128)S(1)}, f32[64,16]{1,0:T(8,128)S(1)}) all-reduce(f32[256]{0:T(256)S(1)} %fusion.19, f32[64]{0:T(128)S(1)} %fusion.23, f32[64,16]{1,0:T(8,128)S(1)} %bitcast.70, f32[64,16]{1,0:T(8,128)S(1)} %fusion.5), channel_id=1, replica_groups=mesh['dp'=64,'group'=8] {'group'}, use_global_device_ids=true, to_apply=%region_2.3 | all-reduce | flops 2368 | bytes 18944 | tf_op jit(solution)/shard_map/psum | solution.py:86
  208.8 13.1 %gather_fusion.5 = bf16[2048]{0:T(1024)(128)(2,1)S(1)} fusion(bf16[1024]{0:T(1024)(128)(2,1)S(1)} %reshape.325, s32[2048]{0:T(1024)S(1)} %broadcast_clamp_fusion.1), kind=kCustom, calls=%fused_computation.5 | custom fusion | bytes 16384 | tf_op jit(solution)/shard_map/gather | solution.py:123
  222.6 6.0 %all-to-all-start.2 = ((bf16[64,1,32]{2,1,0:T(2,128)(2,1)}), bf16[64,1,32]{2,1,0:T(2,128)(2,1)}, u32[]{:S(2)}, u32[]{:S(2)}) async-start(bf16[64,1,32]{2,1,0:T(2,128)(2,1)} %convert_element_type.105), calls=%async_computation.2 | async-start | bytes 65536 | tf_op jit(solution)/shard_map/all_to_all | solution.py:134
  228.6 8.6 %gather_fusion.2 = f32[2048]{0:T(1024)S(1)} fusion(f32[1024]{0:T(1024)S(1)} %reshape.329, s32[2048]{0:T(1024)S(1)} %broadcast_clamp_fusion.1), kind=kCustom, calls=%fused_computation.2 | custom fusion | bytes 24576 | tf_op jit(solution)/shard_map/gather | solution.py:126
  237.3 1.9 fusion.2
  239.2 2.5 all-to-all-done.2
  241.6 12.1 %all-to-all-start.1 = ((bf16[64,32,512]{2,1,0:T(8,128)(2,1)}), bf16[64,32,512]{2,1,0:T(8,128)(2,1)S(1)}, u32[]{:S(2)}, u32[]{:S(2)}) async-start(bf16[64,32,512]{2,1,0:T(8,128)(2,1)} %fusion.2), calls=%async_computation.1 | async-start | bytes 4194304 | tf_op jit(solution)/shard_map/all_to_all | solution.py:131
  257.7 87.9 %all-to-all-done.1 = bf16[64,32,512]{2,1,0:T(8,128)(2,1)S(1)} async-done(((bf16[64,32,512]{2,1,0:T(8,128)(2,1)}), bf16[64,32,512]{2,1,0:T(8,128)(2,1)S(1)}, u32[]{:S(2)}, u32[]{:S(2)}) %all-to-all-start.1) | async-done | bytes 2097184 | tf_op jit(solution)/shard_map/all_to_all | solution.py:131
  346.4 1.6 fusion.9
  348.0 3.1 convolution_convert_fusion
  352.3 40.1 %reduce-scatter.2.cloned.1.call-done = bf16[40,4096]{1,0:T(8,128)(2,1)} async-done(((bf16[320,4096]{1,0:T(8,128)(2,1)}), bf16[40,4096]{1,0:T(8,128)(2,1)}) %reduce-scatter.2.cloned.1.call-update) | async-done | bytes 327696 | tf_op jit(solution)/shard_map/reduce_scatter | solution.py:162
  392.4 1.7 slice.31
  (76 shorter events, 20.2 us)
Async XLA Ops:
  7.2 42.5 %all-gather.2.cloned.1.call-start = ((), (), s32[]{:S(2)}) async-start(), calls=%async_computation.4 | async-start | bytes 2949120 | tf_op jit(solution)/shard_map/all_gather | solution.py:44
  54.2 47.7 %copy-start.1 = (bf16[320,512]{1,0:T(8,128)(2,1)}, bf16[320,512]{1,0:T(8,128)(2,1)S(1)}, u32[]{:S(2)}) copy-start(bf16[320,512]{1,0:T(8,128)(2,1)S(1)} %convolution_convert_fusion.1) | copy-start | bytes 983044
  63.3 112.4 %all-to-all-start = ((bf16[64,32,512]{2,1,0:T(8,128)(2,1)}), bf16[64,32,512]{2,1,0:T(8,128)(2,1)S(1)}, u32[]{:S(2)}, u32[]{:S(2)}) async-start(bf16[64,32,512]{2,1,0:T(8,128)(2,1)} %broadcast_select_fusion), calls=%async_computation | async-start | bytes 4194304 | tf_op jit(solution)/shard_map/all_to_all | solution.py:73
  78.7 127.7 %all-reduce.3.cloned.1.call-start = ((), (), s32[]{:S(2)}) async-start(), calls=%async_computation.5 | async-start | bytes 131072 | tf_op jit(solution)/shard_map/psum | solution.py:86
  205.6 0.5 copy-start.4
  222.6 19.1 %all-to-all-start.2 = ((bf16[64,1,32]{2,1,0:T(2,128)(2,1)}), bf16[64,1,32]{2,1,0:T(2,128)(2,1)}, u32[]{:S(2)}, u32[]{:S(2)}) async-start(bf16[64,1,32]{2,1,0:T(2,128)(2,1)} %convert_element_type.105), calls=%async_computation.2 | async-start | bytes 65536 | tf_op jit(solution)/shard_map/all_to_all | solution.py:134
  228.6 8.7 %copy-start = (bf16[2048,512]{1,0:T(8,128)(2,1)S(1)}, bf16[2048,512]{1,0:T(8,128)(2,1)}, u32[]{:S(2)}) copy-start(bf16[2048,512]{1,0:T(8,128)(2,1)} %gather_fusion.4) | copy-start | bytes 6291460
  239.2 14.9 %copy-start.2 = (f32[64,256]{1,0:T(8,128)S(1)}, f32[64,256]{1,0:T(8,128)}, u32[]{:S(2)}) copy-start(f32[64,256]{1,0:T(8,128)} %all-reduce.3.cloned.1.call-done) | copy-start | bytes 196612
  241.6 104.0 %all-to-all-start.1 = ((bf16[64,32,512]{2,1,0:T(8,128)(2,1)}), bf16[64,32,512]{2,1,0:T(8,128)(2,1)S(1)}, u32[]{:S(2)}, u32[]{:S(2)}) async-start(bf16[64,32,512]{2,1,0:T(8,128)(2,1)} %fusion.2), calls=%async_computation.1 | async-start | bytes 4194304 | tf_op jit(solution)/shard_map/all_to_all | solution.py:131
  253.8 138.6 %reduce-scatter.2.cloned.1.call-start = ((), (), s32[]{:S(2)}) async-start(), calls=%async_computation.6 | async-start | bytes 2949120 | tf_op jit(solution)/shard_map/reduce_scatter | solution.py:162
  345.7 2.3 copy-start.5
  351.0 0.7 copy-start.3
Sparse Core Ops, SparseCore 0:
  10.1 39.5 all-gather.1
  92.8 73.9 all-reduce.2
  351.2 41.1 reduce-scatter.1
where the time goes:
time: 404 us; the launch traced here: 402 us
  waiting for transfers between devices  238 us (59%)
  local copies, waits for them, and re-layouts  61.1 us (15%)
  starting transfers between devices  34 us (8%)
  blocking collectives  25.3 us (6%)
  other arithmetic  15.2 us (4%)
  between operations  14.1 us (3%)
  matrix products  14 us (3%)
    all_to_all x1, waiting for transfers between devices, per_device(): lax.all_to_all(slot_rows.astype(jnp.bfloat16), 'dp', split_axis=0, concat...  87.9 us
    all_to_all x1, waiting for transfers between devices, per_device(): lax.all_to_all(outgoing, 'dp', split_axis=0, concat_axis=0, tiled=True)  73.6 us
    reduce_scatter x1, waiting for transfers between devices, per_device(): lax.psum_scatter(lax.dot_general(stacked, projection, (((1,), (1,)), ((),...  40.1 us
    all_gather x1, waiting for transfers between devices, per_device(): lax.all_gather(own_rows, 'group', axis=0, tiled=True)  34.3 us
    psum x1, blocking collectives, per_device(): lax.psum((inner_in, inner_neg, square_query, square_passage, square_neg),...  25.3 us
    all_to_all x1, starting transfers between devices, per_device(): lax.all_to_all(outgoing, 'dp', split_axis=0, concat_axis=0, tiled=True)  15.3 us
    gather x1, local copies, waits for them, and re-layouts, per_device(): radial_neg[request_of_slot]  13.1 us
    all_to_all x1, starting transfers between devices, per_device(): lax.all_to_all(slot_rows.astype(jnp.bfloat16), 'dp', split_axis=0, concat...  12.1 us
  transfers between devices with their start and end apart: 6, of which 5 were waited for; matrix products, arithmetic and copies ran while one was open for 12% of the time, Pallas kernels for 0%

commit v1 on v0

v1 whole, which is shorter than its diff:
```python
import jax
import jax.numpy as jnp
from jax import lax
from jax.experimental import pallas as pl
from jax.experimental.pallas import tpu as pltpu
from jax.sharding import PartitionSpec as P

TEMPERATURE = 0.05
EPSILON = 1e-06
MESH = pl.DeviceIdType.MESH
F32, BF16, I32 = jnp.float32, jnp.bfloat16, jnp.int32

NZ, NX, NY, NC = 16, 4, 4, 2
NG = NY * NC
D = 4096
COLS = D // NG
QR, PR, PC = 8, 32, 16
GQ, GP = QR * NG, PR * NG
HALF = GP // 2
NEG, CAP = 16, 32
SLOTS = NX * CAP
CHANNELS = 256
SUBS = 2
SUB = GQ // SUBS


def nn(a, b):
    return lax.dot_general(a, b, (((1,), (0,)), ((), ())), preferred_element_type=F32)


def nt(a, b):
    return lax.dot_general(a, b, (((1,), (1,)), ((), ())), preferred_element_type=F32)


def tn(a, b):
    return lax.dot_general(a, b, (((0,), (0,)), ((), ())), preferred_element_type=F32)


def iota(shape, dim):
    return lax.broadcasted_iota(I32, shape, dim)


def eye(rows, columns):
    return (iota((rows, columns), 0) == iota((rows, columns), 1)).astype(F32)


def to_row(column, identity):
    return jnp.sum(identity * column, axis=0, keepdims=True)


def to_column(row, identity):
    return jnp.sum(identity * row, axis=1, keepdims=True)


def kernel(
    qh, ph, weight_hbm, ids_hbm,
    loss_out, qg_out, pg_out,
    wv, idv, hq, hp, qall, pall, code, hits, one_hot, prow,
    pay1, got1, payn, gotn, nz_out, nz_in, nx_out, nx_in, sl_q, sl_p,
    pay2, got2, sum2, fill, w_p, k_c, r_c, t_out, t_in, inv, r_out, r_in,
    zout, zin, cq, gp, xout, xhalf, xfull,
    qpart, qcore, qout, qfull, ppart, pcore, pout, phalf, pfull,
    local_sem, send_sem, recv_sem,
):
    dp, g = lax.axis_index("dp"), lax.axis_index("group")
    z, x = dp // NX, dp % NX
    y, c = g // NC, g % NC

    def at_z(step):
        return (((z + step + 2 * NZ) % NZ) * NX + x, g)

    def at_x(step):
        return (z * NX + (x + step + NX) % NX, g)

    def member(step, other):
        return ((y + step + NY) % NY) * NC + (1 - c if other else c)

    def at_y(step, other=False):
        return (dp, member(step, other))

    others = [(s, o) for s in (0, 1, 2, 3) for o in (False, True) if (s, o) != (0, False)]

    names, departures = {}, {}

    def channel(name):
        return names.setdefault(name, len(names))

    def copy(name, group, src, dst, device):
        return pltpu.make_async_remote_copy(
            src_ref=src, dst_ref=dst, send_sem=send_sem.at[channel(("from", group))],
            recv_sem=recv_sem.at[channel(name)], device_id=device, device_id_type=MESH,
        )

    def send(name, src, dst, device, group=None):
        group = name if group is None else group
        departures.setdefault(group, None)
        copy(name, group, src, dst, device).start()

    def receive(name, dst):
        if name in departures:
            departures[name] = dst
        copy(name, name, dst, dst, at_x(1)).wait_recv()

    def depart():
        for group, ref in list(departures.items()):
            if ref is not None:
                copy(group, group, ref, ref, at_x(1)).wait_send()
                del departures[group]

    w_copies = []
    for k in range(8):
        rows = pl.ds(k * COLS, COLS)
        w_copies.append(pltpu.make_async_copy(weight_hbm.at[rows], wv.at[rows], local_sem.at[2 + k]))
        w_copies[-1].start()
    id_copy = pltpu.make_async_copy(ids_hbm, idv, local_sem.at[1])
    id_copy.start()
    barrier = pltpu.get_barrier_semaphore()
    greeted = [at_z(s) for s in range(1, NZ)] + [at_x(s) for s in range(1, NX)] + [at_y(*o) for o in others]
    for device in greeted:
        pl.semaphore_signal(barrier, inc=1, device_id=device, device_id_type=MESH)
    pl.semaphore_wait(barrier, len(greeted))

    def columns(h):
        return pl.ds(h * (D // 2), D // 2)

    class Gather:
        def __init__(self, name, src, held):
            self.name, self.src, self.held = name, src, held

        def start(self):
            for k in range(2):
                for sign, step in ((0, 1), (1, -1)):
                    h = k if sign == 0 else 1 - k
                    here = self.held.at[g, :, columns(h)]
                    send((self.name, sign, h), self.src.at[:, columns(h)], here, at_y(step))
            send((self.name, "c"), self.src, self.held.at[g], at_y(0, True))
            self.held[pl.ds(g, 1)] = self.src[...][None]

        def forward(self):
            for k in range(2):
                for sign, step in ((0, 1), (1, -1)):
                    h = k if sign == 0 else 1 - k
                    block = member(-step, False)
                    piece = self.held.at[block, :, columns(h)]
                    receive((self.name, sign, h), piece)
                    if k == 0:
                        send((self.name, "far"), piece, piece, at_y(step))
                    else:
                        whole = self.held.at[block]
                        send((self.name, "c"), whole, whole, at_y(0, True))

        def forward_far(self):
            whole = self.held.at[member(2, False)]
            receive((self.name, "far"), whole)
            send((self.name, "c"), whole, whole, at_y(0, True))

        def finish(self):
            receive((self.name, "c"), self.held.at[pl.ds(0, NY)])

    class Near:
        def __init__(self, name, src, held):
            self.name, self.src, self.held = name, src, held

        def start(self):
            for step in (2, 1, 3):
                send((self.name, step), self.src, self.held.at[g], at_y(step))
            send((self.name, "c"), self.src, self.held.at[g], at_y(0, True))
            self.held[pl.ds(g, 1)] = self.src[...][None]

        def forward(self):
            for step in (1, 3, 2):
                block = self.held.at[member(-step, False)]
                receive((self.name, step), block)
                send((self.name, "c"), block, block, at_y(0, True))

        def finish(self):
            receive((self.name, "c"), self.held.at[pl.ds(0, NY)])

    q_gather = Near("q", qh, hq)
    p_gather = [Gather("p%d" % h, ph.at[pl.ds(h * PC, PC)], hp.at[h]) for h in range(2)]

    last = NZ // 2 - 1

    def halved(sign):
        return range(sign * SUBS // 2, (sign + 1) * SUBS // 2)

    def z_piece(sign, s, j):
        block = (z - (1 - 2 * sign) * s + 2 * NZ) % NZ
        return qall.at[block, pl.ds(j * SUB, SUB)]

    def z_step(s):
        for j in range(SUBS):
            for sign in range(2):
                if s < last or j in halved(sign):
                    piece = z_piece(sign, s, j)
                    if s > 0:
                        receive(("z", sign, s - 1, j), piece)
                    send(("z", sign, s, j), piece, piece, at_z(1 - 2 * sign), "z")

    def z_finish():
        for j in range(SUBS):
            for sign in range(2):
                s = last if j in halved(sign) else last - 1
                receive(("z", sign, s, j), z_piece(sign, s + 1, j))
        departures["z"] = qall.at[pl.ds(0, NZ - 1)]

    def x_piece(block, h, half):
        return pall.at[block, pl.ds(h * HALF + half * (HALF // 2), HALF // 2)]

    def x_start(h):
        for k in range(2):
            for sign in range(2):
                half = k if sign == 0 else 1 - k
                piece = x_piece(x, h, half)
                send(("x", h, sign, half), piece, piece, at_x(1 - 2 * sign))

    def x_forward(h):
        for sign in range(2):
            step = 1 - 2 * sign
            piece = x_piece((x - step + NX) % NX, h, sign)
            receive(("x", h, sign, sign), piece)
            send(("x", h, "far"), piece, piece, at_x(step))

    def x_finish(h):
        for sign in range(2):
            step = 1 - 2 * sign
            receive(("x", h, sign, 1 - sign), x_piece((x - step + NX) % NX, h, 1 - sign))
        receive(("x", h, "far"), pall.at[(x + 2) % NX, pl.ds(h * HALF, HALF)])

    def find_slots():
        pieces = []
        for a in range(NZ):
            start = pl.multiple_of(a * NX * GQ + (x // 2) * 2 * GQ, 2 * GQ)
            pieces.append(idv[:, pl.ds(start, 2 * GQ)].astype(F32))
        turned = jnp.concatenate(pieces, axis=0).T
        odd = (x % 2).astype(F32)
        ids = (turned[:GQ] * (1.0 - odd) + turned[GQ:] * odd).astype(I32)
        owner = (ids >> 8) - z * NX
        place = ids & 255
        place = ((place >> 4) & 1) * HALF + (place >> 5) * PC + (place & 15)
        mine = jnp.concatenate([(owner == o).astype(F32) for o in range(NX)], axis=0)
        picked = mine.astype(BF16)
        shape = (NX * GQ, NZ * NEG)
        i, j = iota(shape, 0), iota(shape, 1)
        before = ((i // GQ == j // GQ) & (j < i)).astype(F32).astype(BF16)
        same = i // NEG == j // NEG
        ahead = (same & (i < j)).astype(F32).astype(BF16)
        row_sums = nn(before, picked).astype(BF16)
        rank = nn(row_sums, same.astype(F32).astype(BF16)) + nn(picked, ahead)
        slot = mine * (rank + ((i // GQ) * CAP + 1).astype(F32))
        slot = slot[:GQ] + slot[GQ : 2 * GQ] + slot[2 * GQ : 3 * GQ] + slot[3 * GQ :]
        both = slot.astype(I32) * 256 + place
        both = jnp.where(slot > 0.0, both, 0)
        for a in range(NZ):
            code[a] = both[:, a * NEG : (a + 1) * NEG]

    def fill_slots(first, count):
        def one(a, carry):
            block = code[a]
            lane = iota((GQ, SLOTS), 1) + 1
            hit = jnp.zeros((GQ, SLOTS), F32)
            spot = jnp.zeros((GQ, SLOTS), I32)
            for k in range(NEG):
                column = jnp.broadcast_to(block[:, k : k + 1], (GQ, SLOTS))
                found = (column >> 8) == lane
                hit = jnp.where(found, 1.0, hit)
                spot = jnp.where(found, column & 255, spot)
            hits[a] = hit
            fill[pl.ds(a, 1), :] = jnp.sum(hit, axis=0, keepdims=True)
            row = jnp.sum(spot.astype(F32), axis=0, keepdims=True)
            column = to_column(row, eye(SLOTS, SLOTS)).astype(I32)
            chosen = (iota((SLOTS, GP), 1) == column).astype(F32).astype(BF16)
            for o in range(NX):
                one_hot[o, a] = chosen[o * CAP : (o + 1) * CAP]
            return carry

        lax.fori_loop(first, first + count, one, 0)

    def share(name, pay, got):
        for step, other in others:
            send(name, pay, got.at[g], at_y(step, other))

    def collect(name, pay, got):
        got[pl.ds(g, 1)] = pay[...][None]
        receive(name, got.at[pl.ds(0, NG - 1)])
        total = got[0]
        for i in range(1, NG):
            total = total + got[i]
        return total

    def project_passages(h):
        rows = hp[h].reshape(HALF, D)
        pall[pl.ds(x, 1), h * HALF : (h + 1) * HALF] = nn(rows, wv[...]).astype(BF16)[None]
        x_start(h)

    eye_q, eye_s = eye(GQ, SLOTS), eye(SLOTS, SLOTS)
    p_first, p_second = p_gather

    q_gather.start()
    id_copy.wait()
    find_slots()
    q_gather.forward()
    p_first.start()
    p_second.start()
    fill_slots(0, 6)
    q_gather.finish()
    rows = hq[...].astype(F32).reshape(GQ, D).astype(BF16)
    projected = jnp.zeros((GQ, COLS), F32)
    for k, one in enumerate(w_copies):
        one.wait()
        part = slice(k * COLS, (k + 1) * COLS)
        projected = projected + nn(rows[:, part], wv[part, :])
    qall[pl.ds(z, 1)] = projected.astype(BF16)[None]
    z_step(0)
    p_first.forward()
    fill_slots(6, 2)
    p_second.forward()
    z_step(1)
    p_first.forward_far()
    fill_slots(8, 2)
    p_first.finish()
    z_step(2)
    project_passages(0)
    p_second.forward_far()
    z_step(3)
    p_second.finish()
    project_passages(1)
    z_step(4)

    own_q, own_p = qall[z], pall[x]
    for h in range(2):
        part = own_p[h * HALF : (h + 1) * HALF]
        payn[h : h + 1] = jnp.sum(nt(part, part) * eye_s, axis=0, keepdims=True)
    own_q32 = own_q.astype(F32)
    payn[2:3] = to_row(jnp.sum(own_q32 * own_q32, axis=1, keepdims=True), eye_q)
    payn[3:] = jnp.zeros((payn.shape[0] - 3, SLOTS), F32)
    share("n", payn, gotn)

    inner = nt(own_q, own_p)
    pay1[0:GQ] = inner[:, :SLOTS]
    pay1[GQ:] = inner[:, SLOTS:]
    share("s1", pay1, got1)
    x_forward(0)
    z_step(5)
    fill_slots(10, 4)
    sums = collect("n", payn, gotn)
    square_p = jnp.concatenate([sums[0:1], sums[1:2]], axis=1)
    square_q = to_column(sums[2:3], eye_q)
    nz_out[...] = sums[2:3]
    nx_out[...] = square_p
    nz_in[pl.ds(z, 1)] = sums[2:3][None]
    nx_in[pl.ds(x, 1)] = square_p[None]
    for s in range(1, NX):
        send("nx", nx_out, nx_in.at[x], at_x(s))
    for s in range(1, NZ):
        send("nz", nz_out, nz_in.at[z], at_z(s))
    x_forward(1)
    z_step(6)
    fill_slots(14, 2)
    x_finish(0)
    z_step(7)
    x_finish(1)

    for o in range(NX):
        chosen = nn(one_hot[o].reshape(NZ * CAP, GP), pall[o])
        prow[:, o * CAP : (o + 1) * CAP, :] = chosen.astype(BF16).reshape(NZ, CAP, COLS)

    def by_groups(one, first=0, count=NZ, width=4):
        def some(i, carry):
            for k in range(width):
                one(first + i * width + k)
            return carry

        lax.fori_loop(0, count // width, some, 0)

    def pair_products(step):
        a = (z + step + 2 * NZ) % NZ
        products = nt(qall[a], prow[a])
        pay2[pl.ds(a, 1), :] = jnp.sum(products * hits[a], axis=0, keepdims=True)

    by_groups(pair_products, 2 - NZ // 2, NZ - 4)
    z_finish()
    for step in (NZ // 2 - 2, NZ // 2 - 1, NZ // 2, NZ // 2 + 1):
        pair_products(step)
    share("s2", pay2, got2)

    receive("nx", nx_in.at[pl.ds(0, NX - 1)])
    receive("nz", nz_in.at[pl.ds(0, NZ - 1)])

    depart()

    def slot_norms(a):
        column = to_column(nz_in[a], eye(GQ, SLOTS))
        sl_q[pl.ds(a, 1), :] = jnp.sum(hits[a] * column, axis=0, keepdims=True)
        columns = [
            jnp.sum(one_hot[o, a].astype(F32) * nx_in[o], axis=1, keepdims=True) for o in range(NX)
        ]
        sl_p[pl.ds(a, 1), :] = to_row(jnp.concatenate(columns, axis=0), eye(SLOTS, SLOTS))

    by_groups(slot_norms)

    sums = collect("s1", pay1, got1)
    inner = jnp.concatenate([sums[0:GQ], sums[GQ : 2 * GQ]], axis=1)
    norm = jnp.sqrt(square_q + EPSILON) * jnp.sqrt(square_p + EPSILON)
    cosine = inner / norm
    weight = jnp.exp((cosine - 1.0) / TEMPERATURE)
    weight_sum = jnp.sum(weight, axis=1, keepdims=True)
    spot = iota((GQ, GP), 1)
    passage = ((spot >> 4) & 7) * PR + (spot >> 7) * PC + (spot & 15)
    positive = (passage == iota((GQ, GP), 0) * 4).astype(F32)

    inner_slot = collect("s2", pay2, got2)
    square_slot_p = sl_p[...]
    norm_slot_q = jnp.sqrt(sl_q[...] + EPSILON)
    norm_slot_p = jnp.sqrt(square_slot_p + EPSILON)
    cosine_slot = inner_slot / (norm_slot_q * norm_slot_p)
    weight_slot = jnp.exp((cosine_slot - 1.0) / TEMPERATURE) * fill[...]
    sum2[0:NZ] = weight_slot
    sum2[NZ:] = weight_slot * cosine_slot
    w_p[...] = weight_slot / norm_slot_p
    k_c[...] = weight_slot / (norm_slot_q * norm_slot_p) / TEMPERATURE
    r_c[...] = weight_slot * cosine_slot / (square_slot_p + EPSILON) / TEMPERATURE

    def query_terms(a):
        coefficient = (hits[a] * w_p[pl.ds(a, 1), :]).astype(BF16)
        return nn(coefficient, prow[a])

    def zr_step(s):
        far = query_terms((z + NZ // 2) % NZ) if s == 0 else None
        terms = []
        for sign, step in ((0, 1), (1, -1)):
            block = (z + step * (NZ // 2 - s) + NZ) % NZ
            terms.append(far if s == 0 else query_terms(block))
        for j in range(SUBS):
            for sign, step in ((0, 1), (1, -1)):
                if s == 0 and j not in halved(sign):
                    continue
                value = terms[sign][j * SUB : (j + 1) * SUB]
                if s > 1 or (s == 1 and j in halved(sign)):
                    receive(("zr", sign, s - 1, j), zin.at[sign, s - 1, j])
                    value = value + zin[sign, s - 1, j].astype(F32)
                zout[sign, s, j] = value.astype(BF16)
                send(("zr", sign, s, j), zout.at[sign, s, j], zin.at[sign, s, j], at_z(step), "zr")

    zr_step(0)

    def eye_at(second):
        return (iota((GQ, SLOTS), 1) == iota((GQ, SLOTS), 0) + GQ * second).astype(F32)

    def partial_totals(i):
        row = jnp.zeros((1, SLOTS), F32)
        for second in range(2):
            a = i + second * (NZ // 2)
            column = jnp.sum(hits[a] * sum2[pl.ds(a, 1), :], axis=1, keepdims=True)
            row = row + to_row(column, eye_at(second))
        t_out[pl.ds(i, 1), :] = row

    by_groups(partial_totals, 0, NZ // 2)
    own_row, own_eye = pl.ds(z % (NZ // 2), 1), eye_at(z // (NZ // 2))
    t_out[own_row, :] = t_out[own_row, :] + to_row(weight_sum, own_eye)
    t_in[pl.ds(z, 1)] = t_out[...][None]
    for s in range(1, NZ):
        send("t", t_out, t_in.at[z], at_z(s))
    zr_step(1)

    def partial_radials(a):
        column = jnp.sum(hits[a] * sum2[pl.ds(NZ + a, 1), :], axis=1, keepdims=True)
        r_out[pl.ds(a, 1)] = to_row(column, eye(GQ, SLOTS))[None]

    by_groups(partial_radials)
    r_in[pl.ds(z, 1)] = r_out[pl.ds(z, 1)]
    for s in range(1, NZ):
        send("r", r_out.at[(z + s) % NZ], r_in.at[z], at_z(s))
    zr_step(2)

    receive("t", t_in.at[pl.ds(0, NZ - 1)])
    totals = t_in[0]
    for i in range(1, NZ):
        totals = totals + t_in[i]
    inv[...] = 1.0 / totals

    def passage_terms(a):
        hit, q_rows, p_rows = hits[a], qall[a], prow[a]
        column = to_column(inv[pl.ds(a % (NZ // 2), 1), :], eye_at(a // (NZ // 2)))
        spread = hit * column
        top = spread * k_c[pl.ds(a, 1), :]
        share_of = jnp.sum(spread, axis=0, keepdims=True) * r_c[pl.ds(a, 1), :]
        bottom = eye(SLOTS, SLOTS) * (-share_of)
        lhs = jnp.concatenate([top, bottom], axis=0).astype(BF16)
        terms = tn(lhs, jnp.concatenate([q_rows, p_rows], axis=0)).astype(BF16)
        for o in range(NX):
            cq[o, a] = terms[o * CAP : (o + 1) * CAP]

    by_groups(passage_terms, 0, NZ // 2)
    zr_step(3)
    by_groups(passage_terms, NZ // 2, NZ // 2)
    zr_step(4)

    def passage_sums(step):
        o = (x + step + NX) % NX
        gp[o] = tn(one_hot[o].reshape(NZ * CAP, GP), cq[o].reshape(NZ * CAP, COLS))

    def xr_rows(h, half):
        return slice(h * HALF + half * (HALF // 2), h * HALF + (half + 1) * (HALF // 2))

    def xr_start(h):
        for sign in range(2):
            xout[h, 0, sign] = gp[(x + 2) % NX, xr_rows(h, sign)].astype(BF16)
            send(("xr", h, sign, "far"), xout.at[h, 0, sign], xhalf.at[h, sign], at_x(1 - 2 * sign))

    def xr_own(h):
        for sign in range(2):
            near = (x + 1 - 2 * sign + NX) % NX
            xout[h, 1 + sign, 1 - sign] = gp[near, xr_rows(h, 1 - sign)].astype(BF16)
            there = xfull.at[h, sign, 1 - sign]
            send(("xr", h), xout.at[h, 1 + sign, 1 - sign], there, at_x(1 - 2 * sign))

    def xr_forward(h):
        for sign in range(2):
            near = (x + 1 - 2 * sign + NX) % NX
            receive(("xr", h, sign, "far"), xhalf.at[h, sign])
            merged = gp[near, xr_rows(h, sign)] + xhalf[h, sign].astype(F32)
            xout[h, 1 + sign, sign] = merged.astype(BF16)
            there = xfull.at[h, sign, sign]
            send(("xr", h), xout.at[h, 1 + sign, sign], there, at_x(1 - 2 * sign))

    def xr_finish(h):
        receive(("xr", h), xfull.at[h])
        value = gp[x, h * HALF : (h + 1) * HALF]
        full = xfull[h].reshape(2, HALF, COLS)
        return value + full[0].astype(F32) + full[1].astype(F32)

    class Scatter:
        def __init__(self, name, rows, part, core, out, half, full):
            self.name, self.rows = name, rows
            self.part, self.core, self.out, self.half, self.full = part, core, out, half, full
            self.places = [(y + step) % NY for step in (2, 1, 3, 0)]

        def product(self, down):
            def one(i, carry):
                columns = pl.ds(pl.multiple_of(i * 512, 512), 512)
                block = nt(down, wv[columns, :]).reshape(NY, NC, self.rows, 512)
                for k in range(NC):
                    self.part[k, :, :, columns] = block[:, k].astype(BF16)
                return carry

            lax.fori_loop(0, D // 512, one, 0)
            for i, place in enumerate(self.places):
                there = self.core.at[place]
                send((self.name, "c", i), self.part.at[1 - c, place], there, at_y(0, True))

        def arrive(self, i):
            receive((self.name, "c", i), self.core.at[self.places[i]])

        def both(self, i, h):
            place = self.places[i]
            cut = slice(h * (D // 2), (h + 1) * (D // 2))
            return self.part[c, place, :, cut].astype(F32) + self.core[place, :, cut].astype(F32)

        def start(self):
            self.arrive(0)
            for sign in range(2):
                self.out[0, sign] = self.both(0, sign).astype(BF16)
                there = self.half.at[sign]
                send((self.name, "far", sign), self.out.at[0, sign], there, at_y(1 - 2 * sign))
            for sign in range(2):
                self.arrive(1 + sign)
                self.out[1 + sign, 1 - sign] = self.both(1 + sign, 1 - sign).astype(BF16)
                there = self.full.at[sign, 1 - sign]
                send((self.name, "full"), self.out.at[1 + sign, 1 - sign], there, at_y(1 - 2 * sign))

        def forward(self):
            for sign in range(2):
                merged = self.both(1 + sign, sign)
                receive((self.name, "far", sign), self.half.at[sign])
                self.out[1 + sign, sign] = (merged + self.half[sign].astype(F32)).astype(BF16)
                there = self.full.at[sign, sign]
                send((self.name, "full"), self.out.at[1 + sign, sign], there, at_y(1 - 2 * sign))

        def finish(self, out):
            self.arrive(3)
            own = [self.both(3, h) for h in range(2)]
            receive((self.name, "full"), self.full)
            for h in range(2):
                total = own[h] + self.full[0, h].astype(F32) + self.full[1, h].astype(F32)
                out[:, h * (D // 2) : (h + 1) * (D // 2)] = total.astype(BF16)

    class NearScatter(Scatter):
        def start(self):
            for i, step in enumerate((2, 1, 3)):
                self.arrive(i)
                for h in range(2):
                    self.out[i, h] = self.both(i, h).astype(BF16)
                send((self.name, "near"), self.out.at[i], self.full.at[i], at_y(step))

        def finish(self, out):
            self.arrive(3)
            own = [self.both(3, h) for h in range(2)]
            receive((self.name, "near"), self.full)
            for h in range(2):
                total = own[h] + self.full[0, h].astype(F32)
                total = total + self.full[1, h].astype(F32) + self.full[2, h].astype(F32)
                out[:, h * (D // 2) : (h + 1) * (D // 2)] = total.astype(BF16)

    q_scatter = NearScatter("Q", QR, qpart, qcore, qout, None, qfull)
    p_scatter = [
        Scatter("P%d" % h, PC, ppart.at[h], pcore.at[h], pout.at[h], phalf.at[h], pfull.at[h])
        for h in range(2)
    ]

    passage_sums(2)
    xr_start(0)
    xr_start(1)
    passage_sums(1)
    passage_sums(-1)
    xr_own(0)
    xr_own(1)
    zr_step(5)
    passage_sums(0)

    total = 1.0 / to_column(inv[own_row, :], own_eye)
    inverse = 1.0 / total
    loss = jnp.log(total) + (1.0 - jnp.sum(positive * cosine, axis=1, keepdims=True)) / TEMPERATURE
    mine = (iota((GQ, SLOTS), 0) == g * QR + iota((GQ, SLOTS), 1)).astype(F32)
    loss_out[...] = jnp.sum(mine * loss, axis=0, keepdims=True)
    slope = (weight * inverse - positive) / TEMPERATURE
    pull = slope * cosine
    radial_p = jnp.sum(pull, axis=0, keepdims=True) / (square_p + EPSILON)
    coefficient = (slope / norm).astype(BF16)
    group_p = tn(coefficient, own_q)
    xr_forward(0)
    zr_step(6)
    down_p = []
    eye_p = eye(HALF, HALF)
    for h in range(2):
        column = to_column(radial_p[:, h * HALF : (h + 1) * HALF], eye_p)
        rows = slice(h * HALF, (h + 1) * HALF)
        down_p.append(group_p[rows] - column * own_p[rows].astype(F32))
    xr_forward(1)
    receive("r", r_in.at[pl.ds(0, NZ - 1)])
    radials = r_in[0]
    for i in range(1, NZ):
        radials = radials + r_in[i]
    radial_slots = to_column(radials, eye_q) * inverse / TEMPERATURE
    radial_q = jnp.sum(pull, axis=1, keepdims=True) + radial_slots
    group_q = nn(coefficient, own_p) - (radial_q / (square_q + EPSILON)) * own_q32
    own_terms = query_terms(z)
    zr_step(7)
    p_scatter[0].product((xr_finish(0) + down_p[0]).astype(BF16))

    p_scatter[1].product((xr_finish(1) + down_p[1]).astype(BF16))

    for sign in range(2):
        for j in range(SUBS):
            receive(("zr", sign, last, j), zin.at[sign, last, j])
    departures["zr"] = qall.at[pl.ds(0, NZ - 1)]
    from_z = own_terms + jnp.concatenate(
        [zin[0, last, j].astype(F32) + zin[1, last, j].astype(F32) for j in range(SUBS)], axis=0
    )
    factor = inverse / jnp.sqrt(square_q + EPSILON) / TEMPERATURE
    q_scatter.product((group_q + from_z * factor).astype(BF16))
    p_scatter[0].start()
    p_scatter[1].start()
    q_scatter.start()
    p_scatter[0].forward()
    p_scatter[1].forward()
    p_scatter[0].finish(pg_out.at[0:PC])
    p_scatter[1].finish(pg_out.at[PC:PR])
    q_scatter.finish(qg_out)
    depart()
    assert not departures
    assert len(names) <= CHANNELS


def place_outputs(loss, query_grad, passage_grad, loss_out, query_out, passage_out):
    loss_out[...] = loss[0, :QR]
    query_out[...] = query_grad[...]
    passage_out[...] = passage_grad[...]


def per_device(query_hidden, passage_hidden, projection, negative_ids):
    vmem = pl.BlockSpec(memory_space=pltpu.VMEM)
    hbm = pl.BlockSpec(memory_space=pl.ANY)
    v = pltpu.VMEM
    loss, query_grad, passage_grad = pl.pallas_call(
        kernel,
        out_shape=(
            jax.ShapeDtypeStruct((1, SLOTS), F32),
            jax.ShapeDtypeStruct((QR, D), BF16),
            jax.ShapeDtypeStruct((PR, D), BF16),
        ),
        in_specs=[vmem, vmem, hbm, hbm],
        out_specs=(vmem, vmem, vmem),
        scratch_shapes=[
            v((D, COLS), BF16),
            v((NEG, NZ * NX * GQ), I32),
            v((NG, QR, D), BF16),
            v((2, NG, PC, D), BF16),
            v((NZ, GQ, COLS), BF16),
            v((NX, GP, COLS), BF16),
            v((NZ, GQ, NEG), I32),
            v((NZ, GQ, SLOTS), F32),
            v((NX, NZ, CAP, GP), BF16),
            v((NZ, SLOTS, COLS), BF16),
            v((2 * GQ, SLOTS), F32),
            v((NG, 2 * GQ, SLOTS), F32),
            v((8, SLOTS), F32),
            v((NG, 8, SLOTS), F32),
            v((1, SLOTS), F32),
            v((NZ, 1, SLOTS), F32),
            v((1, GP), F32),
            v((NX, 1, GP), F32),
            v((NZ, SLOTS), F32),
            v((NZ, SLOTS), F32),
            v((NZ, SLOTS), F32),
            v((NG, NZ, SLOTS), F32),
            v((2 * NZ, SLOTS), F32),
            v((NZ, SLOTS), F32),
            v((NZ, SLOTS), F32),
            v((NZ, SLOTS), F32),
            v((NZ, SLOTS), F32),
            v((NZ // 2, SLOTS), F32),
            v((NZ, NZ // 2, SLOTS), F32),
            v((NZ // 2, SLOTS), F32),
            v((NZ, 1, SLOTS), F32),
            v((NZ, 1, SLOTS), F32),
            v((2, NZ // 2, SUBS, SUB, COLS), BF16),
            v((2, NZ // 2, SUBS, SUB, COLS), BF16),
            v((NX, NZ, CAP, COLS), BF16),
            v((NX, GP, COLS), F32),
            v((2, 3, 2, HALF // 2, COLS), BF16),
            v((2, 2, HALF // 2, COLS), BF16),
            v((2, 2, 2, HALF // 2, COLS), BF16),
            v((NC, NY, QR, D), BF16),
            v((NY, QR, D), BF16),
            v((3, 2, QR, D // 2), BF16),
            v((3, 2, QR, D // 2), BF16),
            v((2, NC, NY, PC, D), BF16),
            v((2, NY, PC, D), BF16),
            v((2, 3, 2, PC, D // 2), BF16),
            v((2, 2, PC, D // 2), BF16),
            v((2, 2, 2, PC, D // 2), BF16),
            pltpu.SemaphoreType.DMA((10,)),
            pltpu.SemaphoreType.DMA((CHANNELS,)),
            pltpu.SemaphoreType.DMA((CHANNELS,)),
        ],
        compiler_params=pltpu.CompilerParams(
            collective_id=0, has_side_effects=True, vmem_limit_bytes=56 * 1024 * 1024
        ),
    )(query_hidden, passage_hidden, projection, negative_ids.T)
    return pl.pallas_call(
        place_outputs,
        out_shape=(
            jax.ShapeDtypeStruct((QR,), F32),
            jax.ShapeDtypeStruct((QR, D), BF16),
            jax.ShapeDtypeStruct((PR, D), BF16),
        ),
        in_specs=[vmem, vmem, vmem],
        out_specs=(vmem, vmem, vmem),
    )(loss, query_grad, passage_grad)


def solution(mesh):
    in_specs = (P(("dp", "group"), None), P(("dp", "group"), None), P(None, "group"), P())
    out_specs = (P(("dp", "group")), P(("dp", "group"), None), P(("dp", "group"), None))
    return jax.shard_map(
        per_device, mesh=mesh, in_specs=in_specs, out_specs=out_specs, check_vma=False
    )
```

time: 404 us -> 110 us (0.27)
  waiting for transfers between devices: 238 us -> 0 us
  Pallas kernels: 0 us -> 107 us
  local copies, waits for them, and re-layouts: 61.1 us -> 0 us
  starting transfers between devices: 34 us -> 0 us
  blocking collectives: 25.3 us -> 0 us
  other arithmetic: 15.2 us -> 0 us
  matrix products: 14 us -> 0 us
  between operations: 14.1 us -> 0.64 us
    all_to_all x3 -> x0, waiting for transfers between devices: 164 us -> none  [the longest x1 87.9 us: per_device(): lax.all_to_all(slot_rows.astype(jnp.bfloat16), 'dp', split_axis=0, concat...]
    pallas_call x0 -> x2, Pallas kernels: none -> 107 us  [the longest x1 105 us: per_device(): pl.pallas_call(kernel, out_shape=(jax.ShapeDtypeStruct((1, SLOTS), F32),...]
    gather x6 -> x0, local copies, waits for them, and re-layouts: 50.9 us -> none  [the longest x1 13.1 us: per_device(): radial_neg[request_of_slot]]
    reduce_scatter x1 -> x0, waiting for transfers between devices: 40.1 us -> none  [per_device(): lax.psum_scatter(lax.dot_general(stacked, projection, (((1,), (1,)), ((),...]
    all_gather x1 -> x0, waiting for transfers between devices: 34.3 us -> none  [per_device(): lax.all_gather(own_rows, 'group', axis=0, tiled=True)]
    all_to_all x3 -> x0, starting transfers between devices: 33.4 us -> none  [the longest x1 15.3 us: per_device(): lax.all_to_all(outgoing, 'dp', split_axis=0, concat_axis=0, tiled=True)]
    psum x1 -> x0, blocking collectives: 25.3 us -> none  [per_device(): lax.psum((inner_in, inner_neg, square_query, square_passage, square_neg),...]
    dot_general x11 -> x0, matrix products: 14 us -> none  [the longest x1 4.49 us: per_device(): jnp.dot(lax.all_gather(own_rows, 'group', axis=0, tiled=True), projection...]
  transfers between devices with their start and end apart: 6 -> 0, of which waited for: 5 -> 0; matrix products, arithmetic and copies ran while one was open for 12% -> 0% of each run, Pallas kernels for 0% -> 0%
where the time goes in v1:
time: 110 us; the launch traced here: 108 us
  Pallas kernels  107 us (97%)
    pallas_call x1, Pallas kernels, per_device(): pl.pallas_call(kernel, out_shape=(jax.ShapeDtypeStruct((1, SLOTS), F32),...  105 us

profile of v1, /device:TPU:1, one launch (start us, length us, event | category | flops | bytes accessed | tf_op | source)
XLA Modules:
  0.0 107.7 jit_solution(14506021405396061266)
XLA Ops:
  0.6 105.4 %shard_map.67 = (f32[1,128]{1,0:T(1,128)}, bf16[8,4096]{1,0:T(8,128)(2,1)}, bf16[32,4096]{1,0:T(8,128)(2,1)}) custom-call(bf16[8,4096]{1,0:T(8,128)(2,1)} %qh.1, bf16[32,4096]{1,0:T(8,128)(2,1)} %ph.1, bf16[4096,512]{1,0:T(8,128)(2,1)} %weight_hbm.1, s32[16,4096]{1,0:T(8,128)} %bitcast.1), custom_call_target="tpu_custom_call" | custom-call | tf_op jit(solution)/shard_map/pallas_call | solution.py:685
  106.0 1.7 %shard_map.68 = (f32[8]{0:T(128)}, bf16[8,4096]{1,0:T(8,128)(2,1)}, bf16[32,4096]{1,0:T(8,128)(2,1)}) custom-call(f32[1,128]{1,0:T(1,128)} %get-tuple-element.6.loss, bf16[8,4096]{1,0:T(8,128)(2,1)} %get-tuple-element.7.query_grad, bf16[32,4096]{1,0:T(8,128)(2,1)} %get-tuple-element.8.passage_grad), custom_call_target="tpu_custom_call" | custom-call | tf_op jit(solution)/shard_map/pallas_call | solution.py:751

commit v2 on v1

--- a/solution.py
+++ b/solution.py
@@ -58,7 +58,7 @@
     wv, idv, hq, hp, qall, pall, code, hits, one_hot, prow,
     pay1, got1, payn, gotn, nz_out, nz_in, nx_out, nx_in, sl_q, sl_p,
     pay2, got2, sum2, fill, w_p, k_c, r_c, t_out, t_in, inv, r_out, r_in,
-    zout, zin, cq, gp, xout, xhalf, xfull,
+    zout, zin, turned_k, turned_hot, cq, gp, xout, xhalf, xfull,
     qpart, qcore, qout, qfull, ppart, pcore, pout, phalf, pfull,
     local_sem, send_sem, recv_sem,
 ):
@@ -297,10 +297,10 @@
     p_first, p_second = p_gather
 
     q_gather.start()
+    p_first.start()
     id_copy.wait()
     find_slots()
     q_gather.forward()
-    p_first.start()
     p_second.start()
     fill_slots(0, 6)
     q_gather.finish()
@@ -442,8 +442,6 @@
                 zout[sign, s, j] = value.astype(BF16)
                 send(("zr", sign, s, j), zout.at[sign, s, j], zin.at[sign, s, j], at_z(step), "zr")
 
-    zr_step(0)
-
     def eye_at(second):
         return (iota((GQ, SLOTS), 1) == iota((GQ, SLOTS), 0) + GQ * second).astype(F32)
 
@@ -461,17 +459,15 @@
     t_in[pl.ds(z, 1)] = t_out[...][None]
     for s in range(1, NZ):
         send("t", t_out, t_in.at[z], at_z(s))
+    zr_step(0)
+
+    def turn_terms(a):
+        turned_k[a] = (hits[a] * k_c[pl.ds(a, 1), :]).T.astype(BF16)
+
+    by_groups(turn_terms)
     zr_step(1)
-
-    def partial_radials(a):
-        column = jnp.sum(hits[a] * sum2[pl.ds(NZ + a, 1), :], axis=1, keepdims=True)
-        r_out[pl.ds(a, 1)] = to_row(column, eye(GQ, SLOTS))[None]
-
-    by_groups(partial_radials)
-    r_in[pl.ds(z, 1)] = r_out[pl.ds(z, 1)]
-    for s in range(1, NZ):
-        send("r", r_out.at[(z + s) % NZ], r_in.at[z], at_z(s))
-    zr_step(2)
+    for o in range(NX):
+        turned_hot[o] = one_hot[o].reshape(NZ * CAP, GP).astype(F32).T.astype(BF16)
 
     receive("t", t_in.at[pl.ds(0, NZ - 1)])
     totals = t_in[0]
@@ -480,25 +476,23 @@
     inv[...] = 1.0 / totals
 
     def passage_terms(a):
-        hit, q_rows, p_rows = hits[a], qall[a], prow[a]
         column = to_column(inv[pl.ds(a % (NZ // 2), 1), :], eye_at(a // (NZ // 2)))
-        spread = hit * column
-        top = spread * k_c[pl.ds(a, 1), :]
-        share_of = jnp.sum(spread, axis=0, keepdims=True) * r_c[pl.ds(a, 1), :]
-        bottom = eye(SLOTS, SLOTS) * (-share_of)
-        lhs = jnp.concatenate([top, bottom], axis=0).astype(BF16)
-        terms = tn(lhs, jnp.concatenate([q_rows, p_rows], axis=0)).astype(BF16)
+        scaled = (qall[a].astype(F32) * column).astype(BF16)
+        shares = jnp.sum(hits[a] * column, axis=0, keepdims=True) * r_c[pl.ds(a, 1), :]
+        pulls = (eye(SLOTS, SLOTS) * (-shares)).astype(BF16)
+        lhs = jnp.concatenate([pulls, turned_k[a]], axis=1)
+        terms = nn(lhs, jnp.concatenate([prow[a], scaled], axis=0)).astype(BF16)
         for o in range(NX):
             cq[o, a] = terms[o * CAP : (o + 1) * CAP]
 
     by_groups(passage_terms, 0, NZ // 2)
+    zr_step(2)
+    by_groups(passage_terms, NZ // 2, NZ // 2)
     zr_step(3)
-    by_groups(passage_terms, NZ // 2, NZ // 2)
-    zr_step(4)
 
     def passage_sums(step):
         o = (x + step + NX) % NX
-        gp[o] = tn(one_hot[o].reshape(NZ * CAP, GP), cq[o].reshape(NZ * CAP, COLS))
+        gp[o] = nn(turned_hot[o], cq[o].reshape(NZ * CAP, COLS))
 
     def xr_rows(h, half):
         return slice(h * HALF + half * (HALF // 2), h * HALF + (half + 1) * (HALF // 2))
@@ -536,15 +530,12 @@
             self.part, self.core, self.out, self.half, self.full = part, core, out, half, full
             self.places = [(y + step) % NY for step in (2, 1, 3, 0)]
 
-        def product(self, down):
-            def one(i, carry):
-                columns = pl.ds(pl.multiple_of(i * 512, 512), 512)
-                block = nt(down, wv[columns, :]).reshape(NY, NC, self.rows, 512)
-                for k in range(NC):
-                    self.part[k, :, :, columns] = block[:, k].astype(BF16)
-                return carry
-
-            lax.fori_loop(0, D // 512, one, 0)
+        def part_out(self, block, columns):
+            block = block.reshape(NY, NC, self.rows, 512)
+            for k in range(NC):
+                self.part[k, :, :, columns] = block[:, k].astype(BF16)
+
+        def to_core(self):
             for i, place in enumerate(self.places):
                 there = self.core.at[place]
                 send((self.name, "c", i), self.part.at[1 - c, place], there, at_y(0, True))
@@ -602,6 +593,23 @@
                 total = total + self.full[1, h].astype(F32) + self.full[2, h].astype(F32)
                 out[:, h * (D // 2) : (h + 1) * (D // 2)] = total.astype(BF16)
 
+    def project_back(scatters, downs):
+        down = jnp.concatenate(downs, axis=0)
+
+        def one(i, carry):
+            columns = pl.ds(pl.multiple_of(i * 512, 512), 512)
+            block = nt(down, wv[columns, :])
+            first = 0
+            for scatter in scatters:
+                count = NG * scatter.rows
+                scatter.part_out(block[first : first + count], columns)
+                first += count
+            return carry
+
+        lax.fori_loop(0, D // 512, one, 0)
+        for scatter in scatters:
+            scatter.to_core()
+
     q_scatter = NearScatter("Q", QR, qpart, qcore, qout, None, qfull)
     p_scatter = [
         Scatter("P%d" % h, PC, ppart.at[h], pcore.at[h], pout.at[h], phalf.at[h], pfull.at[h])
@@ -615,8 +623,17 @@
     passage_sums(-1)
     xr_own(0)
     xr_own(1)
-    zr_step(5)
+    zr_step(4)
     passage_sums(0)
+    def partial_radials(a):
+        column = jnp.sum(hits[a] * sum2[pl.ds(NZ + a, 1), :], axis=1, keepdims=True)
+        r_out[pl.ds(a, 1)] = to_row(column, eye(GQ, SLOTS))[None]
+
+    by_groups(partial_radials)
+    r_in[pl.ds(z, 1)] = r_out[pl.ds(z, 1)]
+    for s in range(1, NZ):
+        send("r", r_out.at[(z + s) % NZ], r_in.at[z], at_z(s))
+
 
     total = 1.0 / to_column(inv[own_row, :], own_eye)
     inverse = 1.0 / total
@@ -627,8 +644,10 @@
     pull = slope * cosine
     radial_p = jnp.sum(pull, axis=0, keepdims=True) / (square_p + EPSILON)
     coefficient = (slope / norm).astype(BF16)
+    zr_step(5)
     group_p = tn(coefficient, own_q)
     xr_forward(0)
+    xr_forward(1)
     zr_step(6)
     down_p = []
     eye_p = eye(HALF, HALF)
@@ -636,7 +655,6 @@
         column = to_column(radial_p[:, h * HALF : (h + 1) * HALF], eye_p)
         rows = slice(h * HALF, (h + 1) * HALF)
         down_p.append(group_p[rows] - column * own_p[rows].astype(F32))
-    xr_forward(1)
     receive("r", r_in.at[pl.ds(0, NZ - 1)])
     radials = r_in[0]
     for i in range(1, NZ):
@@ -646,9 +664,9 @@
     group_q = nn(coefficient, own_p) - (radial_q / (square_q + EPSILON)) * own_q32
     own_terms = query_terms(z)
     zr_step(7)
-    p_scatter[0].product((xr_finish(0) + down_p[0]).astype(BF16))
-
-    p_scatter[1].product((xr_finish(1) + down_p[1]).astype(BF16))
+    project_back([p_scatter[0]], [(xr_finish(0) + down_p[0]).astype(BF16)])
+    second_p = (xr_finish(1) + down_p[1]).astype(BF16)
+    p_scatter[0].start()
 
     for sign in range(2):
         for j in range(SUBS):
@@ -658,15 +676,15 @@
         [zin[0, last, j].astype(F32) + zin[1, last, j].astype(F32) for j in range(SUBS)], axis=0
     )
     factor = inverse / jnp.sqrt(square_q + EPSILON) / TEMPERATURE
-    q_scatter.product((group_q + from_z * factor).astype(BF16))
-    p_scatter[0].start()
+    down_q = (group_q + from_z * factor).astype(BF16)
+    project_back([p_scatter[1], q_scatter], [second_p, down_q])
+    p_scatter[0].forward()
     p_scatter[1].start()
     q_scatter.start()
-    p_scatter[0].forward()
+    p_scatter[0].finish(pg_out.at[0:PC])
     p_scatter[1].forward()
-    p_scatter[0].finish(pg_out.at[0:PC])
+    q_scatter.finish(qg_out)
     p_scatter[1].finish(pg_out.at[PC:PR])
-    q_scatter.finish(qg_out)
     depart()
     assert not departures
     assert len(names) <= CHANNELS
@@ -726,6 +744,8 @@
             v((NZ, 1, SLOTS), F32),
             v((2, NZ // 2, SUBS, SUB, COLS), BF16),
             v((2, NZ // 2, SUBS, SUB, COLS), BF16),
+            v((NZ, SLOTS, GQ), BF16),
+            v((NX, GP, NZ * CAP), BF16),
             v((NX, NZ, CAP, COLS), BF16),
             v((NX, GP, COLS), F32),
             v((2, 3, 2, HALF // 2, COLS), BF16),

time: 110 us -> 109 us (level); the launches traced: 108 us -> 109 us
  Pallas kernels: 107 us -> 109 us
    pallas_call x1, Pallas kernels: 105 us -> 107 us  [per_device(): pl.pallas_call(kernel, out_shape=(jax.ShapeDtypeStruct((1, SLOTS), F32),...]
where the time goes in v2:
time: 109 us
  Pallas kernels  109 us (100%)
    pallas_call x1, Pallas kernels, per_device(): pl.pallas_call(kernel, out_shape=(jax.ShapeDtypeStruct((1, SLOTS), F32),...  107 us

profile of v2, /device:TPU:1, one launch (start us, length us, event | category | flops | bytes accessed | tf_op | source)
XLA Modules:
  0.0 109.3 jit_solution(8635010855907161738)
XLA Ops:
  0.6 106.9 %shard_map.67 = (f32[1,128]{1,0:T(1,128)}, bf16[8,4096]{1,0:T(8,128)(2,1)}, bf16[32,4096]{1,0:T(8,128)(2,1)}) custom-call(bf16[8,4096]{1,0:T(8,128)(2,1)} %qh.1, bf16[32,4096]{1,0:T(8,128)(2,1)} %ph.1, bf16[4096,512]{1,0:T(8,128)(2,1)} %weight_hbm.1, s32[16,4096]{1,0:T(8,128)} %bitcast.1), custom_call_target="tpu_custom_call" | custom-call | tf_op jit(solution)/shard_map/pallas_call | solution.py:703
  107.6 1.7 %shard_map.68 = (f32[8]{0:T(128)}, bf16[8,4096]{1,0:T(8,128)(2,1)}, bf16[32,4096]{1,0:T(8,128)(2,1)}) custom-call(f32[1,128]{1,0:T(1,128)} %get-tuple-element.6.loss, bf16[8,4096]{1,0:T(8,128)(2,1)} %get-tuple-element.7.query_grad, bf16[32,4096]{1,0:T(8,128)(2,1)} %get-tuple-element.8.passage_grad), custom_call_target="tpu_custom_call" | custom-call | tf_op jit(solution)/shard_map/pallas_call | solution.py:771

commit v3 on v2

--- a/solution.py
+++ b/solution.py
@@ -179,29 +179,44 @@
     q_gather = Near("q", qh, hq)
     p_gather = [Gather("p%d" % h, ph.at[pl.ds(h * PC, PC)], hp.at[h]) for h in range(2)]
 
-    last = NZ // 2 - 1
+    far = NZ // 2
+    leap = far // 2
 
     def halved(sign):
         return range(sign * SUBS // 2, (sign + 1) * SUBS // 2)
 
-    def z_piece(sign, s, j):
-        block = (z - (1 - 2 * sign) * s + 2 * NZ) % NZ
+    def z_piece(sign, distance, j):
+        block = (z - (1 - 2 * sign) * distance + 2 * NZ) % NZ
         return qall.at[block, pl.ds(j * SUB, SUB)]
 
-    def z_step(s):
+    def z_hop(here, there):
         for j in range(SUBS):
             for sign in range(2):
-                if s < last or j in halved(sign):
-                    piece = z_piece(sign, s, j)
-                    if s > 0:
-                        receive(("z", sign, s - 1, j), piece)
-                    send(("z", sign, s, j), piece, piece, at_z(1 - 2 * sign), "z")
+                if there < far or j in halved(sign):
+                    piece = z_piece(sign, here, j)
+                    if here > 0:
+                        receive(("z", sign, here, j), piece)
+                    target = at_z((1 - 2 * sign) * (there - here))
+                    send(("z", sign, there, j), piece, piece, target, "z")
+
+    def z_step(s):
+        if s == 0:
+            z_hop(0, 1)
+            z_hop(0, leap)
+        else:
+            if s + 1 < leap:
+                z_hop(s, s + 1)
+            z_hop(leap + s - 1, leap + s)
+        if s == leap:
+            for j in range(SUBS):
+                for sign in range(2):
+                    receive(("z", sign, leap - 1, j), z_piece(sign, leap - 1, j))
 
     def z_finish():
         for j in range(SUBS):
             for sign in range(2):
-                s = last if j in halved(sign) else last - 1
-                receive(("z", sign, s, j), z_piece(sign, s + 1, j))
+                distance = far if j in halved(sign) else far - 1
+                receive(("z", sign, distance, j), z_piece(sign, distance, j))
         departures["z"] = qall.at[pl.ds(0, NZ - 1)]
 
     def x_piece(block, h, half):
@@ -302,7 +317,8 @@
     find_slots()
     q_gather.forward()
     p_second.start()
-    fill_slots(0, 6)
+    fill_slots(0, 4)
+    p_first.forward()
     q_gather.finish()
     rows = hq[...].astype(F32).reshape(GQ, D).astype(BF16)
     projected = jnp.zeros((GQ, COLS), F32)
@@ -312,20 +328,17 @@
         projected = projected + nn(rows[:, part], wv[part, :])
     qall[pl.ds(z, 1)] = projected.astype(BF16)[None]
     z_step(0)
-    p_first.forward()
-    fill_slots(6, 2)
     p_second.forward()
+    p_first.forward_far()
+    fill_slots(4, 4)
+    p_first.finish()
+    project_passages(0)
     z_step(1)
-    p_first.forward_far()
+    p_second.forward_far()
     fill_slots(8, 2)
-    p_first.finish()
-    z_step(2)
-    project_passages(0)
-    p_second.forward_far()
-    z_step(3)
     p_second.finish()
     project_passages(1)
-    z_step(4)
+    z_step(2)
 
     own_q, own_p = qall[z], pall[x]
     for h in range(2):
@@ -341,7 +354,7 @@
     pay1[GQ:] = inner[:, SLOTS:]
     share("s1", pay1, got1)
     x_forward(0)
-    z_step(5)
+    z_step(3)
     fill_slots(10, 4)
     sums = collect("n", payn, gotn)
     square_p = jnp.concatenate([sums[0:1], sums[1:2]], axis=1)
@@ -355,10 +368,9 @@
     for s in range(1, NZ):
         send("nz", nz_out, nz_in.at[z], at_z(s))
     x_forward(1)
-    z_step(6)
+    z_step(4)
     fill_slots(14, 2)
     x_finish(0)
-    z_step(7)
     x_finish(1)
 
     for o in range(NX):
@@ -425,22 +437,26 @@
         coefficient = (hits[a] * w_p[pl.ds(a, 1), :]).astype(BF16)
         return nn(coefficient, prow[a])
 
+    def zr_hop(here, there):
+        for sign in range(2):
+            step = 1 - 2 * sign
+            terms = query_terms((z + step * here + NZ) % NZ)
+            for j in range(SUBS):
+                if here == far and j not in halved(sign):
+                    continue
+                value = terms[j * SUB : (j + 1) * SUB]
+                if here not in (far, leap - 1) and (here < far - 1 or j in halved(sign)):
+                    receive(("zr", sign, here + 1, j), zin.at[sign, here, j])
+                    value = value + zin[sign, here, j].astype(F32)
+                zout[sign, here - 1, j] = value.astype(BF16)
+                target = zin.at[sign, here - 1, j]
+                send(("zr", sign, here, j), zout.at[sign, here - 1, j], target, at_z(step * (here - there)), "zr")
+
     def zr_step(s):
-        far = query_terms((z + NZ // 2) % NZ) if s == 0 else None
-        terms = []
-        for sign, step in ((0, 1), (1, -1)):
-            block = (z + step * (NZ // 2 - s) + NZ) % NZ
-            terms.append(far if s == 0 else query_terms(block))
-        for j in range(SUBS):
-            for sign, step in ((0, 1), (1, -1)):
-                if s == 0 and j not in halved(sign):
-                    continue
-                value = terms[sign][j * SUB : (j + 1) * SUB]
-                if s > 1 or (s == 1 and j in halved(sign)):
-                    receive(("zr", sign, s - 1, j), zin.at[sign, s - 1, j])
-                    value = value + zin[sign, s - 1, j].astype(F32)
-                zout[sign, s, j] = value.astype(BF16)
-                send(("zr", sign, s, j), zout.at[sign, s, j], zin.at[sign, s, j], at_z(step), "zr")
+        here = far - s
+        zr_hop(here, here - 1 if here > leap else 0)
+        if s < leap - 1:
+            zr_hop(leap - 1 - s, leap - 2 - s)
 
     def eye_at(second):
         return (iota((GQ, SLOTS), 1) == iota((GQ, SLOTS), 0) + GQ * second).astype(F32)
@@ -644,11 +660,9 @@
     pull = slope * cosine
     radial_p = jnp.sum(pull, axis=0, keepdims=True) / (square_p + EPSILON)
     coefficient = (slope / norm).astype(BF16)
-    zr_step(5)
     group_p = tn(coefficient, own_q)
     xr_forward(0)
     xr_forward(1)
-    zr_step(6)
     down_p = []
     eye_p = eye(HALF, HALF)
     for h in range(2):
@@ -663,27 +677,29 @@
     radial_q = jnp.sum(pull, axis=1, keepdims=True) + radial_slots
     group_q = nn(coefficient, own_p) - (radial_q / (square_q + EPSILON)) * own_q32
     own_terms = query_terms(z)
-    zr_step(7)
+
+    pieces = []
+    for j in range(SUBS):
+        piece = own_terms[j * SUB : (j + 1) * SUB]
+        for sign in range(2):
+            for here in (1, leap):
+                receive(("zr", sign, here, j), zin.at[sign, here - 1, j])
+                piece = piece + zin[sign, here - 1, j].astype(F32)
+        pieces.append(piece)
+    departures["zr"] = qall.at[pl.ds(0, NZ - 1)]
+    factor = inverse / jnp.sqrt(square_q + EPSILON) / TEMPERATURE
+    down_q = (group_q + jnp.concatenate(pieces, axis=0) * factor).astype(BF16)
+    project_back([q_scatter], [down_q])
     project_back([p_scatter[0]], [(xr_finish(0) + down_p[0]).astype(BF16)])
     second_p = (xr_finish(1) + down_p[1]).astype(BF16)
+    q_scatter.start()
+    project_back([p_scatter[1]], [second_p])
     p_scatter[0].start()
-
-    for sign in range(2):
-        for j in range(SUBS):
-            receive(("zr", sign, last, j), zin.at[sign, last, j])
-    departures["zr"] = qall.at[pl.ds(0, NZ - 1)]
-    from_z = own_terms + jnp.concatenate(
-        [zin[0, last, j].astype(F32) + zin[1, last, j].astype(F32) for j in range(SUBS)], axis=0
-    )
-    factor = inverse / jnp.sqrt(square_q + EPSILON) / TEMPERATURE
-    down_q = (group_q + from_z * factor).astype(BF16)
-    project_back([p_scatter[1], q_scatter], [second_p, down_q])
+    p_scatter[1].start()
     p_scatter[0].forward()
-    p_scatter[1].start()
-    q_scatter.start()
-    p_scatter[0].finish(pg_out.at[0:PC])
     p_scatter[1].forward()
     q_scatter.finish(qg_out)
+    p_scatter[0].finish(pg_out.at[0:PC])
     p_scatter[1].finish(pg_out.at[PC:PR])
     depart()
     assert not departures

time: 109 us -> 110 us (level)
  no operation moved by 1% of the time
where the time goes in v3:
time: 110 us
  Pallas kernels  109 us (99%)
    pallas_call x1, Pallas kernels, per_device(): pl.pallas_call(kernel, out_shape=(jax.ShapeDtypeStruct((1, SLOTS), F32),...  107 us

profile of v3, /device:TPU:1, one launch (start us, length us, event | category | flops | bytes accessed | tf_op | source)
XLA Modules:
  0.0 109.5 jit_solution(11724117123644901931)
XLA Ops:
  0.6 107.1 %shard_map.67 = (f32[1,128]{1,0:T(1,128)}, bf16[8,4096]{1,0:T(8,128)(2,1)}, bf16[32,4096]{1,0:T(8,128)(2,1)}) custom-call(bf16[8,4096]{1,0:T(8,128)(2,1)} %qh.1, bf16[32,4096]{1,0:T(8,128)(2,1)} %ph.1, bf16[4096,512]{1,0:T(8,128)(2,1)} %weight_hbm.1, s32[16,4096]{1,0:T(8,128)} %bitcast.1), custom_call_target="tpu_custom_call" | custom-call | tf_op jit(solution)/shard_map/pallas_call | solution.py:719
  107.8 1.7 %shard_map.68 = (f32[8]{0:T(128)}, bf16[8,4096]{1,0:T(8,128)(2,1)}, bf16[32,4096]{1,0:T(8,128)(2,1)}) custom-call(f32[1,128]{1,0:T(1,128)} %get-tuple-element.6.loss, bf16[8,4096]{1,0:T(8,128)(2,1)} %get-tuple-element.7.query_grad, bf16[32,4096]{1,0:T(8,128)(2,1)} %get-tuple-element.8.passage_grad), custom_call_target="tpu_custom_call" | custom-call | tf_op jit(solution)/shard_map/pallas_call | solution.py:787

commit v4 on v3

--- a/solution.py
+++ b/solution.py
@@ -289,7 +289,11 @@
                 one_hot[o, a] = chosen[o * CAP : (o + 1) * CAP]
             return carry
 
-        lax.fori_loop(first, first + count, one, 0)
+        def two(i, carry):
+            one(first + 2 * i, carry)
+            return one(first + 2 * i + 1, carry)
+
+        lax.fori_loop(0, count // 2, two, 0)
 
     def share(name, pay, got):
         for step, other in others:
@@ -377,7 +381,7 @@
         chosen = nn(one_hot[o].reshape(NZ * CAP, GP), pall[o])
         prow[:, o * CAP : (o + 1) * CAP, :] = chosen.astype(BF16).reshape(NZ, CAP, COLS)
 
-    def by_groups(one, first=0, count=NZ, width=4):
+    def by_groups(one, first=0, count=NZ, width=8):
         def some(i, carry):
             for k in range(width):
                 one(first + i * width + k)
@@ -390,7 +394,7 @@
         products = nt(qall[a], prow[a])
         pay2[pl.ds(a, 1), :] = jnp.sum(products * hits[a], axis=0, keepdims=True)
 
-    by_groups(pair_products, 2 - NZ // 2, NZ - 4)
+    by_groups(pair_products, 2 - NZ // 2, NZ - 4, 6)
     z_finish()
     for step in (NZ // 2 - 2, NZ // 2 - 1, NZ // 2, NZ // 2 + 1):
         pair_products(step)
@@ -438,9 +442,11 @@
         return nn(coefficient, prow[a])
 
     def zr_hop(here, there):
+        terms = None
         for sign in range(2):
             step = 1 - 2 * sign
-            terms = query_terms((z + step * here + NZ) % NZ)
+            if here < far or terms is None:
+                terms = query_terms((z + step * here + NZ) % NZ)
             for j in range(SUBS):
                 if here == far and j not in halved(sign):
                     continue
@@ -689,12 +695,12 @@
     departures["zr"] = qall.at[pl.ds(0, NZ - 1)]
     factor = inverse / jnp.sqrt(square_q + EPSILON) / TEMPERATURE
     down_q = (group_q + jnp.concatenate(pieces, axis=0) * factor).astype(BF16)
-    project_back([q_scatter], [down_q])
-    project_back([p_scatter[0]], [(xr_finish(0) + down_p[0]).astype(BF16)])
+    first_p = (xr_finish(0) + down_p[0]).astype(BF16)
+    project_back([p_scatter[0], q_scatter], [first_p, down_q])
     second_p = (xr_finish(1) + down_p[1]).astype(BF16)
-    q_scatter.start()
     project_back([p_scatter[1]], [second_p])
     p_scatter[0].start()
+    q_scatter.start()
     p_scatter[1].start()
     p_scatter[0].forward()
     p_scatter[1].forward()

time: 110 us -> 110 us (level); the launches traced: 110 us -> 108 us
  Pallas kernels: 109 us -> 107 us
    pallas_call x1, Pallas kernels: 107 us -> 106 us  [per_device(): pl.pallas_call(kernel, out_shape=(jax.ShapeDtypeStruct((1, SLOTS), F32),...]
where the time goes in v4:
time: 110 us; the launch traced here: 108 us
  Pallas kernels  107 us (97%)
    pallas_call x1, Pallas kernels, per_device(): pl.pallas_call(kernel, out_shape=(jax.ShapeDtypeStruct((1, SLOTS), F32),...  106 us

profile of v4, /device:TPU:1, one launch (start us, length us, event | category | flops | bytes accessed | tf_op | source)
XLA Modules:
  0.0 108.0 jit_solution(16766956590920857962)
XLA Ops:
  0.6 105.6 %shard_map.67 = (f32[1,128]{1,0:T(1,128)}, bf16[8,4096]{1,0:T(8,128)(2,1)}, bf16[32,4096]{1,0:T(8,128)(2,1)}) custom-call(bf16[8,4096]{1,0:T(8,128)(2,1)} %qh.1, bf16[32,4096]{1,0:T(8,128)(2,1)} %ph.1, bf16[4096,512]{1,0:T(8,128)(2,1)} %weight_hbm.1, s32[16,4096]{1,0:T(8,128)} %bitcast.1), custom_call_target="tpu_custom_call" | custom-call | tf_op jit(solution)/shard_map/pallas_call | solution.py:725
  106.2 1.7 %shard_map.68 = (f32[8]{0:T(128)}, bf16[8,4096]{1,0:T(8,128)(2,1)}, bf16[32,4096]{1,0:T(8,128)(2,1)}) custom-call(f32[1,128]{1,0:T(1,128)} %get-tuple-element.6.loss, bf16[8,4096]{1,0:T(8,128)(2,1)} %get-tuple-element.7.query_grad, bf16[32,4096]{1,0:T(8,128)(2,1)} %get-tuple-element.8.passage_grad), custom_call_target="tpu_custom_call" | custom-call | tf_op jit(solution)/shard_map/pallas_call | solution.py:793

commit v5 on v4

--- a/solution.py
+++ b/solution.py
@@ -317,10 +317,10 @@
 
     q_gather.start()
     p_first.start()
+    p_second.start()
     id_copy.wait()
     find_slots()
     q_gather.forward()
-    p_second.start()
     fill_slots(0, 4)
     p_first.forward()
     q_gather.finish()

time: 110 us -> 110 us (level); the launches traced: 108 us -> 110 us
  Pallas kernels: 107 us -> 109 us
    pallas_call x1, Pallas kernels: 106 us -> 107 us  [per_device(): pl.pallas_call(kernel, out_shape=(jax.ShapeDtypeStruct((1, SLOTS), F32),...]
where the time goes in v5:
time: 110 us
  Pallas kernels  109 us (99%)
    pallas_call x1, Pallas kernels, per_device(): pl.pallas_call(kernel, out_shape=(jax.ShapeDtypeStruct((1, SLOTS), F32),...  107 us

profile of v5, /device:TPU:1, one launch (start us, length us, event | category | flops | bytes accessed | tf_op | source)
XLA Modules:
  0.0 109.6 jit_solution(14963154508511674517)
XLA Ops:
  0.6 107.2 %shard_map.67 = (f32[1,128]{1,0:T(1,128)}, bf16[8,4096]{1,0:T(8,128)(2,1)}, bf16[32,4096]{1,0:T(8,128)(2,1)}) custom-call(bf16[8,4096]{1,0:T(8,128)(2,1)} %qh.1, bf16[32,4096]{1,0:T(8,128)(2,1)} %ph.1, bf16[4096,512]{1,0:T(8,128)(2,1)} %weight_hbm.1, s32[16,4096]{1,0:T(8,128)} %bitcast.1), custom_call_target="tpu_custom_call" | custom-call | tf_op jit(solution)/shard_map/pallas_call | solution.py:725
  107.9 1.7 %shard_map.68 = (f32[8]{0:T(128)}, bf16[8,4096]{1,0:T(8,128)(2,1)}, bf16[32,4096]{1,0:T(8,128)(2,1)}) custom-call(f32[1,128]{1,0:T(1,128)} %get-tuple-element.6.loss, bf16[8,4096]{1,0:T(8,128)(2,1)} %get-tuple-element.7.query_grad, bf16[32,4096]{1,0:T(8,128)(2,1)} %get-tuple-element.8.passage_grad), custom_call_target="tpu_custom_call" | custom-call | tf_op jit(solution)/shard_map/pallas_call | solution.py:793
